TPU v7x, 512 devices: a whole 4x8x8 slice. The times are simulated.
512 devices in a mesh: row: 16 (over z, core), col: 8 (over y), layer: 4 (over x).
Axes of the slice: x: 4, y: 8, z: 8, core: 2. Of those that a mesh axis runs over, the one named last changes fastest.
Arguments:
- slab_panel: bfloat16 [8192, 4, 4096], P('row', 'layer', 'col'), may hold values from -0.59765625 to 0.59765625
- slab_pattern: int32 [32, 4, 16], P('row', 'layer', 'col'), may hold values 0 or 1
- inner_panel: bfloat16 [4, 4096, 4096], P('layer', 'row', 'col'), may hold values from -0.59765625 to 0.59765625
- inner_pattern: int32 [4, 16, 16], P('layer', 'row', 'col'), may hold values 0 or 1
- slab_rows: int32 [32], P('row'), may hold values from 0 to 63
- column_ids: int32 [16], P('col'), may hold values from 0 to 63
Outputs:
- square_slab: bfloat16 [8192, 4096], P('row', ('col', 'layer'))
All inputs are finite; a program needn't handle non-finite values. No bound on the sum of `slab_pattern` or of `inner_pattern` on one device may be relied on, other than what follows from the above.
Results may differ from a plain program's by a relative error of at most 0.001.
Values may be sent and summed in bfloat16 or wider, within the bound.
A program may use at most 64 MiB of HBM per device.

v0:
```python
import jax
import jax.numpy as jnp
from jax import lax
from jax.sharding import PartitionSpec as P


def apply_pattern(panel, pattern):
    blocks_down, blocks_across = pattern.shape
    block_width = panel.shape[0] // blocks_down
    spread = (
        panel.reshape(blocks_down, block_width, blocks_across, block_width)
        * pattern.astype(panel.dtype)[:, None, :, None]
    )
    return spread.reshape(panel.shape)


def cell_dot(left_rows, right_cols):
    return jnp.dot(left_rows, right_cols, preferred_element_type=jnp.float32)


def tile_product(left_rows, right_cols):
    return cell_dot(left_rows, right_cols)


def on_device(slab_panel, slab_pattern, inner_panel, inner_pattern, slab_rows, column_ids):
    block_width = inner_panel.shape[1] // inner_pattern.shape[1]
    slab_masked = apply_pattern(slab_panel[:, 0, :], slab_pattern[:, 0, :])
    inner_masked = apply_pattern(inner_panel[0], inner_pattern[0])
    keep_cells = column_ids[None, :] >= slab_rows[:, None]
    gathered = lax.all_gather(inner_masked, "row", axis=0, tiled=True)
    tile_sum = tile_product(lax.all_gather(slab_masked, "col", axis=1, tiled=True), gathered)
    layer_count = lax.axis_size("layer")
    share_width = tile_sum.shape[1] // layer_count
    layer_pos = lax.axis_index("layer")
    own_share = lax.psum_scatter(tile_sum, "layer", scatter_dimension=1, tiled=True)
    col_block = (layer_pos * share_width + jnp.arange(share_width, dtype=jnp.int32)) // block_width
    selector = (
        col_block[:, None] == jnp.arange(keep_cells.shape[1], dtype=jnp.int32)[None, :]
    ).astype(jnp.float32)
    keep_cols = jnp.dot(keep_cells.astype(jnp.float32), selector.T)
    blocks_down = keep_cells.shape[0]
    keep_full = jnp.broadcast_to(
        keep_cols[:, None, :], (blocks_down, block_width, share_width)
    ).reshape(blocks_down * block_width, share_width)
    return (own_share * keep_full).astype(jnp.bfloat16)


def solution(mesh):
    return jax.shard_map(
        on_device,
        mesh=mesh,
        in_specs=(
            P("row", "layer", "col"),
            P("row", "layer", "col"),
            P("layer", "row", "col"),
            P("layer", "row", "col"),
            P("row"),
            P("col"),
        ),
        out_specs=P("row", ("col", "layer")),
        check_vma=False,
    )
```

profile of v0, /device:TPU:1, one launch (start us, length us, event | category | flops | bytes accessed | tf_op | source)
XLA Modules:
  0.0 159.6 jit_solution(17145226882084236671)
XLA Ops:
  6.5 0.0 all-gather.3.cloned.1.call-start
  6.5 0.7 convert_element_type.27
  7.2 0.3 mul.32
  7.6 0.1 copy.8
  7.7 1.9 %bitcast_multiply_fusion = bf16[512,512]{1,0:T(8,128)(2,1)} fusion(bf16[512,512]{1,0:T(8,128)(2,1)S(1)} %bitcast.21, bf16[512,1,512]{2,0,1:T(8,128)(2,1)} %param.6), kind=kLoop, calls=%fused_computation | loop fusion | flops 262144 | bytes 1572864 | tf_op jit(solution)/shard_map/mul | solution.py:11
  9.6 0.0 all-gather.3.cloned.1.call-update
  9.6 0.0 all-gather.5.cloned.1.call-start
  9.7 0.7 convert_bitcast_fusion
  10.3 0.1 broadcast_bitcast_fusion
  10.4 1.7 %bitcast_multiply_fusion.2 = bf16[256,512]{1,0:T(8,128)(2,1)} fusion(bf16[1,256,512]{2,1,0:T(8,128)(2,1)} %param.8, bf16[512]{0:T(512)(128)(2,1)S(1)} %bitcast.23), kind=kLoop, calls=%fused_computation.3 | loop fusion | flops 131072 | bytes 525312 | tf_op jit(solution)/shard_map/mul | solution.py:11
  12.1 0.0 all-gather.5.cloned.1.call-update
  12.1 0.0 copy-start
  12.2 0.0 copy-start.1
  12.2 0.0 reduce-scatter.2.cloned.1.call-start
  12.2 60.2 %all-gather.3.cloned.1.call-done = bf16[512,4096]{1,0:T(8,128)(2,1)} async-done(((bf16[512,512]{1,0:T(8,128)(2,1)}), bf16[512,4096]{1,0:T(8,128)(2,1)}) %all-gather.3.cloned.1.call-update) | async-done | bytes 4194320 | tf_op jit(solution)/shard_map/all_gather | solution.py:31
  72.4 47.3 %all-gather.5.cloned.1.call-done = bf16[4096,512]{1,0:T(8,128)(2,1)} async-done(((bf16[256,512]{1,0:T(8,128)(2,1)}), bf16[4096,512]{1,0:T(8,128)(2,1)}) %all-gather.5.cloned.1.call-update) | async-done | bytes 4194320 | tf_op jit(solution)/shard_map/all_gather | solution.py:30
  119.7 6.8 %fusion.6 = f32[512,512]{1,0:T(8,128)} fusion(bf16[512,4096]{1,0:T(8,128)(2,1)} %all-gather.3.cloned.1.call-done, bf16[4096,512]{1,0:T(8,128)(2,1)} %all-gather.5.cloned.1.call-done), kind=kOutput, calls=%fused_computation.17 | convolution fusion | flops 2147483648 | bytes 9437184 | tf_op jit(solution)/shard_map/dot_general | solution.py:18
  126.5 0.0 reduce-scatter.2.cloned.1.call-update
  126.6 0.0 copy-done
  126.6 0.0 copy-done.1
  126.6 0.2 fusion.1
  126.8 24.6 %reduce-scatter.2.cloned.1.call-done = f32[512,128]{1,0:T(8,128)} async-done(((f32[512,512]{1,0:T(8,128)}), f32[512,128]{1,0:T(8,128)}) %reduce-scatter.2.cloned.1.call-update) | async-done | bytes 262160 | tf_op jit(solution)/shard_map/reduce_scatter | solution.py:35
  151.5 1.6 %fusion = bf16[512,128]{1,0:T(8,128)(2,1)} fusion(f32[512,128]{1,0:T(8,128)} %reduce-scatter.2.cloned.1.call-done, f32[2,128]{1,0:T(2,128)S(1)} %fusion.1), kind=kLoop, calls=%fused_computation.2 | loop fusion | flops 131072 | bytes 394240 | tf_op jit(solution)/shard_map/convert_element_type | solution.py:45
  (3 shorter events, 0.0 us)
Async XLA Ops:
  6.5 65.9 %all-gather.3.cloned.1.call-start = ((), (), s32[]{:S(2)}) async-start(), calls=%async_computation.1 | async-start | bytes 4718592 | tf_op jit(solution)/shard_map/all_gather | solution.py:31
  9.6 110.1 %all-gather.5.cloned.1.call-start = ((), (), s32[]{:S(2)}) async-start(), calls=%async_computation.2 | async-start | bytes 4456448 | tf_op jit(solution)/shard_map/all_gather | solution.py:30
  12.1 114.4 %copy-start = (s32[2]{0:T(128)S(1)}, s32[2]{0:T(128)}, u32[]{:S(2)}) copy-start(s32[2]{0:T(128)} %param.11) | copy-start | bytes 28
  12.2 114.4 %copy-start.1 = (s32[2]{0:T(128)S(1)}, s32[2]{0:T(128)}, u32[]{:S(2)}) copy-start(s32[2]{0:T(128)} %param.10) | copy-start | bytes 28
  12.2 139.3 %reduce-scatter.2.cloned.1.call-start = ((), (), s32[]{:S(2)}) async-start(), calls=%async_computation.3 | async-start | bytes 1310720 | tf_op jit(solution)/shard_map/reduce_scatter | solution.py:35
Sparse Core Ops, SparseCore 0:
  9.7 62.6 all-gather.2
  74.5 45.1 all-gather.4
  126.7 24.7 reduce-scatter.1
where the time goes:
time: 161 us; the launch traced here: 160 us
  waiting for transfers between devices  132 us (82%)
  between operations  13.2 us (8%)
  matrix products  7.05 us (4%)
  other arithmetic  6.61 us (4%)
    all_gather x1, waiting for transfers between devices, on_device(): lax.all_gather(slab_masked, 'col', axis=1, tiled=True)  60.2 us
    all_gather x1, waiting for transfers between devices, on_device(): gathered = lax.all_gather(inner_masked, 'row', axis=0, tiled=True)  47.3 us
    reduce_scatter x1, waiting for transfers between devices, on_device(): lax.psum_scatter(tile_sum, 'layer', scatter_dimension=1, tiled=True)  24.6 us
    dot_general x1, matrix products, cell_dot(): return jnp.dot(left_rows, right_cols, preferred_element_type=jnp.float32)  6.85 us
    mul x2, other arithmetic, apply_pattern(): panel.reshape(blocks_down, block_width, blocks_across, block_width)  3.64 us
  transfers between devices with their start and end apart: 3, of which 3 were waited for; matrix products, arithmetic and copies ran while one was open for 2% of the time, Pallas kernels for 0%

commit v1 on v0

v1 whole, which is shorter than its diff:
```python
import functools

import jax
import jax.numpy as jnp
from jax import lax
from jax.experimental import pallas as pl
from jax.experimental.pallas import tpu as pltpu
from jax.sharding import PartitionSpec as P

MESH = pl.DeviceIdType.MESH
BW = 256
NY, NZ, NX = 8, 8, 4
Q = 4
PIECE = 512 // Q
HALF = PIECE // 2
PHASES = 2


def kernel(slab, slab_pat, inner, inner_pat, rows_ids, col_ids, out,
           a_raw, b_raw, a_all, b_all, acc, rs,
           ld_sem, as_sem, ar_sem, bs_sem, br_sem, ss_sem, sr_sem, cs_sem, cr_sem):
    r, y, x = lax.axis_index("row"), lax.axis_index("col"), lax.axis_index("layer")
    z, c = r // 2, r % 2

    def dev(row=r, col=y, layer=x):
        return (row, col, layer)

    y_to = [dev(col=(y + 1) % NY), dev(col=(y + NY - 1) % NY)]
    z_to = [dev(row=((z + 1) % NZ) * 2 + c), dev(row=((z + NZ - 1) % NZ) * 2 + c)]
    sib = dev(row=z * 2 + 1 - c)
    x_to = [dev(layer=(x + d) % NX) for d in range(1, NX)]

    barrier = pltpu.get_barrier_semaphore()
    for peer in y_to + z_to + [sib] + x_to:
        pl.semaphore_signal(barrier, inc=1, device_id=peer, device_id_type=MESH)

    loads = []
    for q in range(Q):
        rows = pl.ds(q * PIECE, PIECE)
        loads.append(pltpu.make_async_copy(slab.at[rows], a_raw.at[rows], ld_sem.at[q]))
    loads.append(pltpu.make_async_copy(inner, b_raw, ld_sem.at[Q]))
    for cp in (loads[0], loads[4], loads[1], loads[2], loads[3]):
        cp.start()

    def mask_a(q):
        loads[q].wait()
        for j in range(2):
            keep = slab_pat[q * PIECE // BW, 0, j].astype(jnp.float32).astype(jnp.bfloat16)
            blk = a_raw[pl.ds(q * PIECE, PIECE), pl.ds(j * BW, BW)]
            a_all[y, pl.ds(q * PIECE, PIECE), pl.ds(j * BW, BW)] = blk * keep

    def mask_b():
        loads[Q].wait()
        for j in range(2):
            keep = inner_pat[0, 0, j].astype(jnp.float32).astype(jnp.bfloat16)
            b_all[z, pl.ds(c * BW, BW), pl.ds(j * BW, BW)] = b_raw[:, pl.ds(j * BW, BW)] * keep

    def y_src(way, d):
        return (y + NY - d) % NY if way == 0 else (y + d) % NY

    def a_copy(way, q, d):
        src = y_src(way, d)
        lo, n = (q * PIECE, PIECE) if d < 3 else (q * PIECE + way * HALF, HALF)
        ref = a_all.at[src, pl.ds(lo, n)]
        return pltpu.make_async_remote_copy(
            src_ref=ref, dst_ref=ref, send_sem=as_sem.at[way, q, d], recv_sem=ar_sem.at[way, q, d],
            device_id=y_to[way], device_id_type=MESH)

    def a_arrive(way, q, d):
        src = y_src(way, d)
        lo, n = (q * PIECE, PIECE) if d < 4 else (q * PIECE + way * HALF, HALF)
        ref = a_all.at[src, pl.ds(lo, n)]
        pltpu.make_async_remote_copy(
            src_ref=ref, dst_ref=ref, send_sem=as_sem.at[way, q, d - 1], recv_sem=ar_sem.at[way, q, d - 1],
            device_id=y_to[way], device_id_type=MESH).wait_recv()

    def z_src(way, d):
        return (z + NZ - d) % NZ if way == 0 else (z + d) % NZ

    def b_ref(way, d, core, part):
        lo, n = (0, BW) if not part else (way * (BW // 2), BW // 2)
        return b_all.at[z_src(way, d), pl.ds(core * BW + lo, n)]

    def b_copy(way, d):
        ref = b_ref(way, d, c, d == 3)
        return pltpu.make_async_remote_copy(
            src_ref=ref, dst_ref=ref, send_sem=bs_sem.at[way, d], recv_sem=br_sem.at[way, d],
            device_id=z_to[way], device_id_type=MESH)

    def b_arrive(way, d):
        ref = b_ref(way, d, c, d == 4)
        pltpu.make_async_remote_copy(
            src_ref=ref, dst_ref=ref, send_sem=bs_sem.at[way, d - 1], recv_sem=br_sem.at[way, d - 1],
            device_id=z_to[way], device_id_type=MESH).wait_recv()

    def s_copy(way, d, core):
        ref = b_ref(way, d, core, d == 4)
        return pltpu.make_async_remote_copy(
            src_ref=ref, dst_ref=ref, send_sem=ss_sem.at[way, d], recv_sem=sr_sem.at[way, d],
            device_id=sib, device_id_type=MESH)

    def c_copy(ph, d):
        return pltpu.make_async_remote_copy(
            src_ref=acc.at[ph, (x + d) % NX], dst_ref=rs.at[ph, d - 1],
            send_sem=cs_sem.at[ph, d - 1], recv_sem=cr_sem.at[ph, d - 1],
            device_id=x_to[d - 1], device_id_type=MESH)

    def mm(ph, src, first=False):
        res = jnp.dot(a_all[src, pl.ds(ph * BW, BW), :], b_all[src], preferred_element_type=jnp.float32)
        for k in range(NX):
            part = res[:, k * 128:(k + 1) * 128]
            if first:
                acc[ph, k] = part
            else:
                acc[ph, k] += part

    def finish(ph):
        for d in range(1, NX):
            c_copy(ph, d).wait_recv()
        total = acc[ph, x] + rs[ph, 0] + rs[ph, 1] + rs[ph, 2]
        keep = col_ids[x // 2] >= rows_ids[ph]
        out[pl.ds(ph * BW, BW), :] = jnp.where(keep, total, 0.0).astype(jnp.bfloat16)

    def a_events(pair, d):
        for q in pair:
            for way in range(2):
                a_arrive(way, q, d)
                if d < 4:
                    a_copy(way, q, d).start()

    def b_events(d):
        for way in range(2):
            b_arrive(way, d)
            if d < 4:
                b_copy(way, d).start()
            s_copy(way, d, c).start()

    mask_a(0)
    pl.semaphore_wait(barrier, 2 + 2 + 1 + NX - 1)
    for way in range(2):
        a_copy(way, 0, 0).start()
    mask_b()
    for way in range(2):
        b_copy(way, 0).start()
    s_copy(0, 0, c).start()
    mask_a(1)
    for way in range(2):
        a_copy(way, 1, 0).start()
    mask_a(2)
    mask_a(3)

    a_events((0, 1), 1)
    b_events(1)
    a_events((0, 1), 2)
    for q in (2, 3):
        for way in range(2):
            a_copy(way, q, 0).start()
    b_events(2)
    a_events((0, 1), 3)
    b_events(3)
    a_events((0, 1), 4)
    a_events((2, 3), 1)
    b_events(4)
    s_copy(0, 0, 1 - c).wait_recv()
    for d in range(1, 5):
        for way in range(2):
            s_copy(way, d, 1 - c).wait_recv()
    mm(0, y, True)
    for d in range(1, 4):
        for way in range(2):
            mm(0, y_src(way, d))
    mm(0, y_src(0, 4))
    for d in range(1, NX):
        c_copy(0, d).start()
    a_events((2, 3), 2)
    mm(1, y, True)
    for d in range(1, 3):
        for way in range(2):
            mm(1, y_src(way, d))
    a_events((2, 3), 3)
    for way in range(2):
        mm(1, y_src(way, 3))
    finish(0)
    a_events((2, 3), 4)
    mm(1, y_src(0, 4))
    for d in range(1, NX):
        c_copy(1, d).start()
    for way in range(2):
        for q in range(Q):
            for d in range(4):
                a_copy(way, q, d).wait_send()
        for d in range(4):
            b_copy(way, d).wait_send()
        for d in range(1, 5):
            s_copy(way, d, c).wait_send()
    s_copy(0, 0, c).wait_send()
    for ph in range(PHASES):
        for d in range(1, NX):
            c_copy(ph, d).wait_send()
    finish(1)


def on_device(slab_panel, slab_pattern, inner_panel, inner_pattern, slab_rows, column_ids):
    any_spec = pl.BlockSpec(memory_space=pl.ANY)
    smem = pl.BlockSpec(memory_space=pltpu.SMEM)
    dma = pltpu.SemaphoreType.DMA
    return pl.pallas_call(
        kernel,
        out_shape=jax.ShapeDtypeStruct((512, 128), jnp.bfloat16),
        in_specs=[any_spec, smem, any_spec, smem, smem, smem],
        out_specs=pl.BlockSpec(memory_space=pltpu.VMEM),
        scratch_shapes=[
            pltpu.VMEM((512, 512), jnp.bfloat16),
            pltpu.VMEM((256, 512), jnp.bfloat16),
            pltpu.VMEM((NY, 512, 512), jnp.bfloat16),
            pltpu.VMEM((NZ, 512, 512), jnp.bfloat16),
            pltpu.VMEM((PHASES, NX, 256, 128), jnp.float32),
            pltpu.VMEM((PHASES, NX - 1, 256, 128), jnp.float32),
            dma((Q + 1,)),
            dma((2, Q, 4)), dma((2, Q, 4)),
            dma((2, 4)), dma((2, 4)),
            dma((2, 5)), dma((2, 5)),
            dma((PHASES, NX - 1)), dma((PHASES, NX - 1)),
        ],
        compiler_params=pltpu.CompilerParams(
            collective_id=0, has_side_effects=True, vmem_limit_bytes=40 * 1024 * 1024),
        cost_estimate=pl.CostEstimate(flops=2 * 512 * 512 * 4096, bytes_accessed=2 << 20, transcendentals=0),
    )(slab_panel.reshape(512, 512), slab_pattern, inner_panel.reshape(256, 512), inner_pattern, slab_rows, column_ids)


def solution(mesh):
    return jax.shard_map(
        on_device,
        mesh=mesh,
        in_specs=(
            P("row", "layer", "col"),
            P("row", "layer", "col"),
            P("layer", "row", "col"),
            P("layer", "row", "col"),
            P("row"),
            P("col"),
        ),
        out_specs=P("row", ("col", "layer")),
        check_vma=False,
    )
```

time: 161 us -> 69.1 us (0.43)
  the two profiles are of different devices: /device:TPU:1 before, /device:TPU:24 now
where the time goes in v1:
time: 69.1 us; the launch traced here: 68.9 us
  Pallas kernels  65.5 us (95%)
  local copies, waits for them, and re-layouts  3.35 us (5%)
    pallas_call x1, Pallas kernels, on_device(): pl.pallas_call(kernel, out_shape=jax.ShapeDtypeStruct((512, 128), jnp.bfl...  65.5 us
    unnamed x13, local copies, waits for them, and re-layouts  3.35 us

profile of v1, /device:TPU:24, one launch (start us, length us, event | category | flops | bytes accessed | tf_op | source)
XLA Modules:
  0.0 68.9 jit_solution(152970469130459892)
XLA Ops:
  0.0 0.0 copy-start.4
  0.0 0.0 copy-start.5
  0.0 0.0 copy-start.2
  0.0 0.0 copy-start.3
  0.0 0.6 copy-done.4
  0.7 0.0 copy-done.5
  0.7 0.0 copy-done.2
  0.7 0.0 copy-done.3
  0.7 0.0 copy-start
  0.7 1.0 %copy-done = bf16[512,1,512]{2,0,1:T(8,128)(2,1)S(1)} copy-done((bf16[512,1,512]{2,0,1:T(8,128)(2,1)S(1)}, bf16[512,1,512]{2,0,1:T(8,128)(2,1)}, u32[]{:S(2)}) %copy-start) | copy-done | bytes 524312
  1.8 0.0 copy-start.1
  1.8 0.9 %copy-done.1 = bf16[1,256,512]{2,1,0:T(8,128)(2,1)S(1)} copy-done((bf16[1,256,512]{2,1,0:T(8,128)(2,1)S(1)}, bf16[1,256,512]{2,1,0:T(8,128)(2,1)}, u32[]{:S(2)}) %copy-start.1) | copy-done | bytes 262168
  2.7 65.5 %shard_map.64 = bf16[512,128]{1,0:T(8,128)(2,1)S(1)} custom-call(bf16[512,512]{1,0:T(8,128)(2,1)S(1)} %bitcast.2, s32[2,1,2]{2,1,0:T(1,128)S(1)} %copy-done.2, bf16[256,512]{1,0:T(8,128)(2,1)S(1)} %bitcast.3, s32[1,1,2]{2,1,0:T(1,128)S(1)} %copy-done.3, s32[2]{0:T(128)S(1)} %copy-done.4, s32[2]{0:T(128)S(1)} %copy-done.5), custom_call_target="tpu_custom_call" | custom-call | flops 2147483648 | bytes 2097152 | tf_op jit(solution)/shard_map/pallas_call | solution.py:207
  68.2 0.7 copy.8
Async XLA Ops:
  0.0 0.7 copy-start.4
  0.0 0.7 copy-start.5
  0.0 0.7 %copy-start.2 = (s32[2,1,2]{2,1,0:T(1,128)S(1)}, s32[2,1,2]{2,1,0:T(1,128)}, u32[]{:S(2)}) copy-start(s32[2,1,2]{2,1,0:T(1,128)} %slab_pat.1) | copy-start | bytes 52
  0.0 0.7 %copy-start.3 = (s32[1,1,2]{2,1,0:T(1,128)S(1)}, s32[1,1,2]{2,1,0:T(1,128)}, u32[]{:S(2)}) copy-start(s32[1,1,2]{2,1,0:T(1,128)} %inner_pat.1) | copy-start | bytes 28
  0.7 1.0 %copy-start = (bf16[512,1,512]{2,0,1:T(8,128)(2,1)S(1)}, bf16[512,1,512]{2,0,1:T(8,128)(2,1)}, u32[]{:S(2)}) copy-start(bf16[512,1,512]{2,0,1:T(8,128)(2,1)} %param.6) | copy-start | bytes 1572868
  1.8 0.9 %copy-start.1 = (bf16[1,256,512]{2,1,0:T(8,128)(2,1)S(1)}, bf16[1,256,512]{2,1,0:T(8,128)(2,1)}, u32[]{:S(2)}) copy-start(bf16[1,256,512]{2,1,0:T(8,128)(2,1)} %param.8) | copy-start | bytes 786436

commit v2 on v0

v2 whole, which is shorter than its diff:
```python
import jax
import jax.numpy as jnp
from jax import lax
from jax.experimental import pallas as pl
from jax.experimental.pallas import tpu as pltpu
from jax.sharding import PartitionSpec as P

MESH = pl.DeviceIdType.MESH
BW = 256
NY, NZ, NX = 8, 8, 4
SIDE = 512
PIECES = (128, 128, 128, 128)
STARTS = tuple(sum(PIECES[:q]) for q in range(len(PIECES)))
Q = len(PIECES)
PB = 2
BP = BW // PB


def kernel(slab, slab_pat, inner, inner_pat, row_ids, col_ids, out,
           a_raw, b_raw, a_all, b_all, acc, rs,
           ld_sem, as_sem, ar_sem, bs_sem, br_sem, ss_sem, sr_sem, cs_sem, cr_sem):
    r, y, x = lax.axis_index("row"), lax.axis_index("col"), lax.axis_index("layer")
    z, c = r // 2, r % 2
    y_to = [(r, (y + 1) % NY, x), (r, (y + NY - 1) % NY, x)]
    z_to = [(((z + 1) % NZ) * 2 + c, y, x), (((z + NZ - 1) % NZ) * 2 + c, y, x)]
    sibling = (z * 2 + 1 - c, y, x)
    x_to = [(r, y, (x + d) % NX) for d in range(1, NX)]
    peers = y_to + z_to + [sibling] + x_to

    barrier = pltpu.get_barrier_semaphore()
    for peer in peers:
        pl.semaphore_signal(barrier, inc=1, device_id=peer, device_id_type=MESH)

    def spans(q):
        for i in range(SIDE // BW):
            lo, hi = max(STARTS[q], i * BW), min(STARTS[q] + PIECES[q], (i + 1) * BW)
            if lo < hi:
                yield i, lo, hi - lo

    loads = [
        pltpu.make_async_copy(slab.at[pl.ds(STARTS[q], n)], a_raw.at[pl.ds(STARTS[q], n)], ld_sem.at[q])
        for q, n in enumerate(PIECES)
    ] + [pltpu.make_async_copy(inner, b_raw, ld_sem.at[Q])]
    for i in [0, Q] + list(range(1, Q)):
        loads[i].start()

    def mask_slab(q):
        loads[q].wait()
        for i, lo, n in spans(q):
            for j in range(SIDE // BW):
                keep = slab_pat[i, 0, j].astype(jnp.float32).astype(jnp.bfloat16)
                at = (pl.ds(lo, n), pl.ds(j * BW, BW))
                a_all[(y, *at)] = a_raw[at] * keep

    def mask_inner():
        loads[Q].wait()
        for j in range(SIDE // BW):
            keep = inner_pat[0, 0, j].astype(jnp.float32).astype(jnp.bfloat16)
            cols = pl.ds(j * BW, BW)
            b_all[z, pl.ds(c * BW, BW), cols] = b_raw[:, cols] * keep

    def source(me, size, way, d):
        return (me + size - d) % size if way == 0 else (me + d) % size

    sends = []

    def start(copy):
        copy.start()
        sends.append(copy)

    def slab_copy(way, q, d, hop):
        n = PIECES[q] if hop < 3 else PIECES[q] // 2
        lo = STARTS[q] + (way * n if hop == 3 else 0)
        ref = a_all.at[source(y, NY, way, d), pl.ds(lo, n)]
        return pltpu.make_async_remote_copy(
            src_ref=ref, dst_ref=ref, send_sem=as_sem.at[way, q, hop], recv_sem=ar_sem.at[way, q, hop],
            device_id=y_to[way], device_id_type=MESH)

    def inner_ref(p, way, d, core, half):
        n = BP // 2 if half else BP
        lo = core * BW + p * BP + (way * n if half else 0)
        return b_all.at[source(z, NZ, way, d), pl.ds(lo, n)]

    def inner_copy(p, way, d, hop):
        ref = inner_ref(p, way, d, c, hop == 3)
        return pltpu.make_async_remote_copy(
            src_ref=ref, dst_ref=ref, send_sem=bs_sem.at[p, way, hop], recv_sem=br_sem.at[p, way, hop],
            device_id=z_to[way], device_id_type=MESH)

    def core_copy(p, way, d, core):
        ref = inner_ref(p, way, d, core, d == 4)
        return pltpu.make_async_remote_copy(
            src_ref=ref, dst_ref=ref, send_sem=ss_sem.at[p, way, d], recv_sem=sr_sem.at[p, way, d],
            device_id=sibling, device_id_type=MESH)

    def part_copy(q, d):
        rows = pl.ds(STARTS[q], PIECES[q])
        return pltpu.make_async_remote_copy(
            src_ref=acc.at[(x + d) % NX, rows], dst_ref=rs.at[d - 1, rows],
            send_sem=cs_sem.at[q, d - 1], recv_sem=cr_sem.at[q, d - 1],
            device_id=x_to[d - 1], device_id_type=MESH)

    def send_slab(q):
        mask_slab(q)
        for way in range(2):
            start(slab_copy(way, q, 0, 0))

    def send_inner():
        mask_inner()
        for p in range(PB):
            for way in range(2):
                start(inner_copy(p, way, 0, 0))
        for p in range(PB):
            start(core_copy(p, 0, 0, c))

    def pass_slab(q, d):
        for way in range(2):
            slab_copy(way, q, d, d - 1).wait_recv()
            if d < 4:
                start(slab_copy(way, q, d, d))

    def pass_inner(p, d):
        for way in range(2):
            inner_copy(p, way, d, d - 1).wait_recv()
            if d < 4:
                start(inner_copy(p, way, d, d))
            start(core_copy(p, way, d, c))

    def wait_core():
        for d in range(5):
            for way in range(2 if d else 1):
                for p in range(PB):
                    core_copy(p, way, d, 1 - c).wait_recv()

    def multiply(q0, nq, d):
        rows = pl.ds(STARTS[q0], sum(PIECES[q0:q0 + nq]))
        for way in range(2 if 0 < d < 4 else 1):
            src = source(y, NY, way, d)
            product = jnp.dot(a_all[src, rows, :], b_all[src], preferred_element_type=jnp.float32)
            for k in range(NX):
                part = product[:, k * 128:(k + 1) * 128]
                acc[k, rows] = part if d == 0 else acc[k, rows] + part

    def send_parts(q):
        for d in (2, 1, 3):
            start(part_copy(q, d))

    def finish(q):
        for d in range(1, NX):
            part_copy(q, d).wait_recv()
        for i, lo, n in spans(q):
            rows = pl.ds(lo, n)
            total = acc[x, rows] + rs[0, rows] + rs[1, rows] + rs[2, rows]
            keep = col_ids[x // 2] >= row_ids[i]
            out[rows, :] = jnp.where(keep, total, 0.0).astype(jnp.bfloat16)

    mask_slab(0)
    pl.semaphore_wait(barrier, len(peers))
    for way in range(2):
        start(slab_copy(way, 0, 0, 0))
    send_slab(1)
    send_inner()
    send_slab(2)
    send_slab(3)
    pass_slab(0, 1)
    pass_inner(0, 1)
    pass_slab(1, 1)
    pass_inner(1, 1)
    pass_slab(2, 1)
    pass_inner(0, 2)
    pass_slab(3, 1)
    pass_inner(1, 2)
    pass_slab(0, 2)
    pass_inner(0, 3)
    pass_slab(1, 2)
    pass_inner(1, 3)
    pass_inner(0, 4)
    pass_inner(1, 4)
    pass_slab(2, 2)
    pass_slab(3, 2)
    wait_core()
    for d in range(3):
        multiply(0, 2, d)
    pass_slab(0, 3)
    multiply(0, 1, 3)
    pass_slab(1, 3)
    multiply(1, 1, 3)
    for d in range(3):
        multiply(2, 2, d)
    pass_slab(0, 4)
    multiply(0, 1, 4)
    send_parts(0)
    pass_slab(2, 3)
    multiply(2, 1, 3)
    pass_slab(1, 4)
    multiply(1, 1, 4)
    send_parts(1)
    pass_slab(3, 3)
    multiply(3, 1, 3)
    pass_slab(2, 4)
    multiply(2, 1, 4)
    send_parts(2)
    pass_slab(3, 4)
    multiply(3, 1, 4)
    send_parts(3)
    for q in range(Q - 1):
        finish(q)
    for copy in sends:
        copy.wait_send()
    finish(Q - 1)


def on_device(slab_panel, slab_pattern, inner_panel, inner_pattern, slab_rows, column_ids):
    whole = pl.BlockSpec(memory_space=pl.ANY)
    scalars = pl.BlockSpec(memory_space=pltpu.SMEM)
    dma = pltpu.SemaphoreType.DMA
    return pl.pallas_call(
        kernel,
        out_shape=jax.ShapeDtypeStruct((SIDE, 128), jnp.bfloat16),
        in_specs=[whole, scalars, whole, scalars, scalars, scalars],
        out_specs=pl.BlockSpec(memory_space=pltpu.VMEM),
        scratch_shapes=[
            pltpu.VMEM((SIDE, SIDE), jnp.bfloat16),
            pltpu.VMEM((BW, SIDE), jnp.bfloat16),
            pltpu.VMEM((NY, SIDE, SIDE), jnp.bfloat16),
            pltpu.VMEM((NZ, SIDE, SIDE), jnp.bfloat16),
            pltpu.VMEM((NX, SIDE, 128), jnp.float32),
            pltpu.VMEM((NX - 1, SIDE, 128), jnp.float32),
            dma((Q + 1,)),
            dma((2, Q, 4)), dma((2, Q, 4)),
            dma((PB, 2, 4)), dma((PB, 2, 4)),
            dma((PB, 2, 5)), dma((PB, 2, 5)),
            dma((Q, NX - 1)), dma((Q, NX - 1)),
        ],
        compiler_params=pltpu.CompilerParams(
            collective_id=0, has_side_effects=True, vmem_limit_bytes=60 * 1024 * 1024),
    )(slab_panel.reshape(SIDE, SIDE), slab_pattern, inner_panel.reshape(BW, SIDE), inner_pattern,
      slab_rows, column_ids)


def solution(mesh):
    return jax.shard_map(
        on_device,
        mesh=mesh,
        in_specs=(
            P("row", "layer", "col"),
            P("row", "layer", "col"),
            P("layer", "row", "col"),
            P("layer", "row", "col"),
            P("row"),
            P("col"),
        ),
        out_specs=P("row", ("col", "layer")),
        check_vma=False,
    )
```

time: 161 us -> 66.8 us (0.41)
  waiting for transfers between devices: 132 us -> 0 us
  Pallas kernels: 0 us -> 65 us
  between operations: 13.2 us -> 0.01 us
  matrix products: 7.05 us -> 0 us
  other arithmetic: 6.61 us -> 0 us
    all_gather x2 -> x0, waiting for transfers between devices: 107 us -> none  [the longest x1 60.2 us: on_device(): lax.all_gather(slab_masked, 'col', axis=1, tiled=True)]
    pallas_call x0 -> x1, Pallas kernels: none -> 65 us  [on_device(): pl.pallas_call(kernel, out_shape=jax.ShapeDtypeStruct((SIDE, 128), jnp.bf...]
    reduce_scatter x1 -> x0, waiting for transfers between devices: 24.6 us -> none  [on_device(): lax.psum_scatter(tile_sum, 'layer', scatter_dimension=1, tiled=True)]
    dot_general x2 -> x0, matrix products: 7.05 us -> none  [the longest x1 6.85 us: cell_dot(): return jnp.dot(left_rows, right_cols, preferred_element_type=jnp.float32)]
    mul x2 -> x0, other arithmetic: 3.64 us -> none  [apply_pattern(): panel.reshape(blocks_down, block_width, blocks_across, block_width)]
    convert_element_type x3 -> x0, other arithmetic: 2.96 us -> none  [the longest x1 1.62 us: on_device(): return (own_share * keep_full).astype(jnp.bfloat16)]
  transfers between devices with their start and end apart: 3 -> 0, of which waited for: 3 -> 0; matrix products, arithmetic and copies ran while one was open for 2% -> 0% of each run, Pallas kernels for 0% -> 0%
where the time goes in v2:
time: 66.8 us; the launch traced here: 66.6 us
  Pallas kernels  65 us (97%)
  local copies, waits for them, and re-layouts  1.57 us (2%)
    pallas_call x1, Pallas kernels, on_device(): pl.pallas_call(kernel, out_shape=jax.ShapeDtypeStruct((SIDE, 128), jnp.bf...  65 us
    unnamed x1, local copies, waits for them, and re-layouts  1.57 us

profile of v2, /device:TPU:1, one launch (start us, length us, event | category | flops | bytes accessed | tf_op | source)
XLA Modules:
  0.0 66.6 jit_solution(13600879884033894595)
XLA Ops:
  0.0 65.0 %shard_map.64 = bf16[512,128]{1,0:T(8,128)(2,1)} custom-call(bf16[512,512]{1,0:T(8,128)(2,1)} %bitcast.2, s32[2,1,2]{2,1,0:T(1,128)} %slab_pat.1, bf16[256,512]{1,0:T(8,128)(2,1)} %bitcast.3, s32[1,1,2]{2,1,0:T(1,128)} %inner_pat.1, s32[2]{0:T(128)} %row_ids.1, s32[2]{0:T(128)} %col_ids.1), custom_call_target="tpu_custom_call" | custom-call | tf_op jit(solution)/shard_map/pallas_call | solution.py:217
  65.0 1.6 %copy.8 = bf16[512,128]{1,0:T(8,128)(2,1)} copy(bf16[512,128]{1,0:T(8,128)(2,1)} %shard_map.64) | data formatting | bytes 262144

commit v3 on v2

--- a/solution.py
+++ b/solution.py
@@ -233,7 +233,7 @@
             dma((Q, NX - 1)), dma((Q, NX - 1)),
         ],
         compiler_params=pltpu.CompilerParams(
-            collective_id=0, has_side_effects=True, vmem_limit_bytes=60 * 1024 * 1024),
+            collective_id=0, has_side_effects=True, vmem_limit_bytes=54976 * 1024),
     )(slab_panel.reshape(SIDE, SIDE), slab_pattern, inner_panel.reshape(BW, SIDE), inner_pattern,
       slab_rows, column_ids)
 

time: 66.8 us -> 65.8 us (0.985)
  Pallas kernels: 65 us -> 64.3 us
    pallas_call x1, Pallas kernels: 65 us -> 64.3 us  [on_device(): pl.pallas_call(kernel, out_shape=jax.ShapeDtypeStruct((SIDE, 128), jnp.bf...]
    unnamed x1 -> x9, local copies, waits for them, and re-layouts: 1.57 us -> 1.36 us
where the time goes in v3:
time: 65.8 us; the launch traced here: 65.6 us
  Pallas kernels  64.3 us (98%)
  local copies, waits for them, and re-layouts  1.36 us (2%)
    pallas_call x1, Pallas kernels, on_device(): pl.pallas_call(kernel, out_shape=jax.ShapeDtypeStruct((SIDE, 128), jnp.bf...  64.3 us
    unnamed x9, local copies, waits for them, and re-layouts  1.36 us

profile of v3, /device:TPU:1, one launch (start us, length us, event | category | flops | bytes accessed | tf_op | source)
XLA Modules:
  0.0 65.6 jit_solution(15168587183906151753)
XLA Ops:
  0.0 0.0 copy-start.2
  0.0 0.0 copy-start.3
  0.0 0.0 copy-start
  0.0 0.0 copy-start.1
  0.0 0.6 copy-done.2
  0.7 0.0 copy-done.3
  0.7 0.0 copy-done
  0.7 0.0 copy-done.1
  0.7 64.3 %shard_map.64 = bf16[512,128]{1,0:T(8,128)(2,1)S(1)} custom-call(bf16[512,512]{1,0:T(8,128)(2,1)} %bitcast.2, s32[2,1,2]{2,1,0:T(1,128)S(1)} %copy-done, bf16[256,512]{1,0:T(8,128)(2,1)} %bitcast.3, s32[1,1,2]{2,1,0:T(1,128)S(1)} %copy-done.1, s32[2]{0:T(128)S(1)} %copy-done.2, s32[2]{0:T(128)S(1)} %copy-done.3), custom_call_target="tpu_custom_call" | custom-call | tf_op jit(solution)/shard_map/pallas_call | solution.py:217
  65.0 0.7 %copy.8 = bf16[512,128]{1,0:T(8,128)(2,1)} copy(bf16[512,128]{1,0:T(8,128)(2,1)S(1)} %shard_map.64) | data formatting | bytes 262144
Async XLA Ops:
  0.0 0.7 copy-start.2
  0.0 0.7 %copy-start.3 = (s32[2]{0:T(128)S(1)}, s32[2]{0:T(128)}, u32[]{:S(2)}) copy-start(s32[2]{0:T(128)} %col_ids.1) | copy-start | bytes 28
  0.0 0.7 %copy-start = (s32[2,1,2]{2,1,0:T(1,128)S(1)}, s32[2,1,2]{2,1,0:T(1,128)}, u32[]{:S(2)}) copy-start(s32[2,1,2]{2,1,0:T(1,128)} %slab_pat.1) | copy-start | bytes 52
  0.0 0.7 %copy-start.1 = (s32[1,1,2]{2,1,0:T(1,128)S(1)}, s32[1,1,2]{2,1,0:T(1,128)}, u32[]{:S(2)}) copy-start(s32[1,1,2]{2,1,0:T(1,128)} %inner_pat.1) | copy-start | bytes 28

commit v4 on v3

--- a/solution.py
+++ b/solution.py
@@ -15,21 +15,53 @@
 PB = 2
 BP = BW // PB
 
+FINISH = (
+    ("slab", 0, 4), ("multiply", 0, 1, 4), ("parts", 0),
+    ("slab", 2, 3), ("multiply", 2, 1, 3),
+    ("slab", 1, 4), ("multiply", 1, 1, 4), ("parts", 1),
+    ("slab", 3, 3), ("multiply", 3, 1, 3),
+    ("slab", 2, 4), ("multiply", 2, 1, 4), ("parts", 2),
+    ("slab", 3, 4), ("multiply", 3, 1, 4), ("parts", 3),
+    ("finish", 0), ("finish", 1), ("finish", 2), ("end",), ("finish", 3),
+)
+OTHER_PLANES = (
+    ("enter",), ("first_slab",), ("send_slab", 1), ("send_inner",), ("send_slab", 2), ("send_slab", 3),
+    ("slab", 0, 1), ("inner", 0, 1), ("slab", 1, 1), ("inner", 1, 1),
+    ("slab", 2, 1), ("inner", 0, 2), ("slab", 3, 1), ("inner", 1, 2),
+    ("slab", 0, 2), ("inner", 0, 3), ("slab", 1, 2), ("inner", 1, 3),
+    ("inner", 0, 4), ("inner", 1, 4), ("slab", 2, 2), ("slab", 3, 2), ("wait_core",),
+    ("multiply", 0, 2, 0), ("multiply", 0, 2, 1), ("multiply", 0, 2, 2),
+    ("slab", 0, 3), ("multiply", 0, 1, 3), ("slab", 1, 3), ("multiply", 1, 1, 3),
+    ("multiply", 2, 2, 0), ("multiply", 2, 2, 1), ("multiply", 2, 2, 2),
+) + FINISH
+FIRST_PLANE = (
+    ("enter_first",), ("first_slab",), ("send_slab", 1), ("send_slab", 2), ("send_slab", 3),
+    ("slab", 0, 1), ("meet",), ("send_inner",), ("slab", 1, 1), ("slab", 2, 1), ("slab", 3, 1),
+    ("inner", 0, 1), ("slab", 0, 2), ("inner", 1, 1), ("slab", 1, 2), ("inner", 0, 2), ("inner", 1, 2),
+    ("slab", 2, 2), ("slab", 3, 2), ("inner", 0, 3), ("slab", 0, 3), ("inner", 1, 3),
+    ("inner", 0, 4), ("slab", 1, 3), ("inner", 1, 4), ("wait_core",),
+    ("multiply", 0, 4, 0), ("multiply", 0, 4, 1), ("multiply", 0, 4, 2), ("multiply", 0, 2, 3),
+) + FINISH
+
 
 def kernel(slab, slab_pat, inner, inner_pat, row_ids, col_ids, out,
            a_raw, b_raw, a_all, b_all, acc, rs,
-           ld_sem, as_sem, ar_sem, bs_sem, br_sem, ss_sem, sr_sem, cs_sem, cr_sem):
+           meet_sem, ld_sem, as_sem, ar_sem, bs_sem, br_sem, ss_sem, sr_sem, cs_sem, cr_sem):
     r, y, x = lax.axis_index("row"), lax.axis_index("col"), lax.axis_index("layer")
     z, c = r // 2, r % 2
     y_to = [(r, (y + 1) % NY, x), (r, (y + NY - 1) % NY, x)]
     z_to = [(((z + 1) % NZ) * 2 + c, y, x), (((z + NZ - 1) % NZ) * 2 + c, y, x)]
     sibling = (z * 2 + 1 - c, y, x)
     x_to = [(r, y, (x + d) % NX) for d in range(1, NX)]
-    peers = y_to + z_to + [sibling] + x_to
-
     barrier = pltpu.get_barrier_semaphore()
-    for peer in peers:
+    for peer in y_to + [sibling] + x_to:
         pl.semaphore_signal(barrier, inc=1, device_id=peer, device_id_type=MESH)
+    near = len(y_to) + 1 + len(x_to)
+    for step in (1, NZ - 1):
+        @pl.when(jnp.logical_and(z != 0, (z + step) % NZ != 0))
+        def _(step=step):
+            pl.semaphore_signal(
+                barrier, inc=1, device_id=(((z + step) % NZ) * 2 + c, y, x), device_id_type=MESH)
 
     def spans(q):
         for i in range(SIDE // BW):
@@ -154,60 +186,46 @@
             keep = col_ids[x // 2] >= row_ids[i]
             out[rows, :] = jnp.where(keep, total, 0.0).astype(jnp.bfloat16)
 
-    mask_slab(0)
-    pl.semaphore_wait(barrier, len(peers))
-    for way in range(2):
-        start(slab_copy(way, 0, 0, 0))
-    send_slab(1)
-    send_inner()
-    send_slab(2)
-    send_slab(3)
-    pass_slab(0, 1)
-    pass_inner(0, 1)
-    pass_slab(1, 1)
-    pass_inner(1, 1)
-    pass_slab(2, 1)
-    pass_inner(0, 2)
-    pass_slab(3, 1)
-    pass_inner(1, 2)
-    pass_slab(0, 2)
-    pass_inner(0, 3)
-    pass_slab(1, 2)
-    pass_inner(1, 3)
-    pass_inner(0, 4)
-    pass_inner(1, 4)
-    pass_slab(2, 2)
-    pass_slab(3, 2)
-    wait_core()
-    for d in range(3):
-        multiply(0, 2, d)
-    pass_slab(0, 3)
-    multiply(0, 1, 3)
-    pass_slab(1, 3)
-    multiply(1, 1, 3)
-    for d in range(3):
-        multiply(2, 2, d)
-    pass_slab(0, 4)
-    multiply(0, 1, 4)
-    send_parts(0)
-    pass_slab(2, 3)
-    multiply(2, 1, 3)
-    pass_slab(1, 4)
-    multiply(1, 1, 4)
-    send_parts(1)
-    pass_slab(3, 3)
-    multiply(3, 1, 3)
-    pass_slab(2, 4)
-    multiply(2, 1, 4)
-    send_parts(2)
-    pass_slab(3, 4)
-    multiply(3, 1, 4)
-    send_parts(3)
-    for q in range(Q - 1):
-        finish(q)
-    for copy in sends:
-        copy.wait_send()
-    finish(Q - 1)
+    def end():
+        for copy in sends:
+            copy.wait_send()
+
+    def enter_first():
+        mask_slab(0)
+        pl.semaphore_wait(barrier, near)
+        for peer in z_to:
+            pl.semaphore_signal(barrier, inc=1, device_id=peer, device_id_type=MESH)
+
+    def enter():
+        mask_slab(0)
+        pl.semaphore_wait(barrier, near + 2)
+
+        for step in (1, NZ - 1):
+            @pl.when((z + step) % NZ == 0)
+            def _(step=step):
+                pl.semaphore_signal(
+                    meet_sem, inc=1, device_id=(((z + step) % NZ) * 2 + c, y, x), device_id_type=MESH)
+
+    def meet():
+        pl.semaphore_wait(meet_sem, 2)
+
+    def first_slab():
+        for way in range(2):
+            start(slab_copy(way, 0, 0, 0))
+
+    steps = {
+        "enter_first": enter_first, "enter": enter, "meet": meet, "first_slab": first_slab,
+        "send_slab": send_slab, "send_inner": send_inner, "slab": pass_slab, "inner": pass_inner,
+        "wait_core": wait_core, "multiply": multiply, "parts": send_parts, "finish": finish, "end": end,
+    }
+
+    def run(schedule):
+        sends.clear()
+        for name, *args in schedule:
+            steps[name](*args)
+
+    pl.when(z == 0)(lambda: run(FIRST_PLANE))
+    pl.when(z != 0)(lambda: run(OTHER_PLANES))
 
 
 def on_device(slab_panel, slab_pattern, inner_panel, inner_pattern, slab_rows, column_ids):
@@ -226,6 +244,7 @@
             pltpu.VMEM((NZ, SIDE, SIDE), jnp.bfloat16),
             pltpu.VMEM((NX, SIDE, 128), jnp.float32),
             pltpu.VMEM((NX - 1, SIDE, 128), jnp.float32),
+            pltpu.SemaphoreType.REGULAR,
             dma((Q + 1,)),
             dma((2, Q, 4)), dma((2, Q, 4)),
             dma((PB, 2, 4)), dma((PB, 2, 4)),

time: 65.8 us -> 61.8 us (0.939)
  the two profiles are of different devices: /device:TPU:1 before, /device:TPU:64 now
where the time goes in v4:
time: 61.8 us; the launch traced here: 61.7 us
  Pallas kernels  60.3 us (98%)
  local copies, waits for them, and re-layouts  1.36 us (2%)
    pallas_call x1, Pallas kernels, on_device(): pl.pallas_call(kernel, out_shape=jax.ShapeDtypeStruct((SIDE, 128), jnp.bf...  60.3 us
    unnamed x9, local copies, waits for them, and re-layouts  1.36 us

profile of v4, /device:TPU:64, one launch (start us, length us, event | category | flops | bytes accessed | tf_op | source)
XLA Modules:
  0.0 61.7 jit_solution(12476869072188658912)
XLA Ops:
  0.0 0.0 copy-start.2
  0.0 0.0 copy-start.3
  0.0 0.0 copy-start
  0.0 0.0 copy-start.1
  0.0 0.6 %copy-done.2 = s32[2]{0:T(128)S(1)} copy-done((s32[2]{0:T(128)S(1)}, s32[2]{0:T(128)}, u32[]{:S(2)}) %copy-start.2) | copy-done | bytes 32
  0.7 0.0 copy-done.3
  0.7 0.0 copy-done
  0.7 0.0 copy-done.1
  0.7 60.3 %shard_map.64 = bf16[512,128]{1,0:T(8,128)(2,1)S(1)} custom-call(bf16[512,512]{1,0:T(8,128)(2,1)} %bitcast.2, s32[2,1,2]{2,1,0:T(1,128)S(1)} %copy-done, bf16[256,512]{1,0:T(8,128)(2,1)} %bitcast.3, s32[1,1,2]{2,1,0:T(1,128)S(1)} %copy-done.1, s32[2]{0:T(128)S(1)} %copy-done.2, s32[2]{0:T(128)S(1)} %copy-done.3), custom_call_target="tpu_custom_call" | custom-call | tf_op jit(solution)/shard_map/pallas_call | solution.py:235
  61.0 0.7 %copy.8 = bf16[512,128]{1,0:T(8,128)(2,1)} copy(bf16[512,128]{1,0:T(8,128)(2,1)S(1)} %shard_map.64) | data formatting | bytes 262144
Async XLA Ops:
  0.0 0.7 %copy-start.2 = (s32[2]{0:T(128)S(1)}, s32[2]{0:T(128)}, u32[]{:S(2)}) copy-start(s32[2]{0:T(128)} %row_ids.1) | copy-start | bytes 28
  0.0 0.7 %copy-start.3 = (s32[2]{0:T(128)S(1)}, s32[2]{0:T(128)}, u32[]{:S(2)}) copy-start(s32[2]{0:T(128)} %col_ids.1) | copy-start | bytes 28
  0.0 0.7 %copy-start = (s32[2,1,2]{2,1,0:T(1,128)S(1)}, s32[2,1,2]{2,1,0:T(1,128)}, u32[]{:S(2)}) copy-start(s32[2,1,2]{2,1,0:T(1,128)} %slab_pat.1) | copy-start | bytes 52
  0.0 0.7 %copy-start.1 = (s32[1,1,2]{2,1,0:T(1,128)S(1)}, s32[1,1,2]{2,1,0:T(1,128)}, u32[]{:S(2)}) copy-start(s32[1,1,2]{2,1,0:T(1,128)} %inner_pat.1) | copy-start | bytes 28

commit v5 on v4

--- a/solution.py
+++ b/solution.py
@@ -16,7 +16,7 @@
 BP = BW // PB
 
 FINISH = (
-    ("slab", 0, 4), ("multiply", 0, 1, 4), ("parts", 0),
+    ("slab", 0, 4), ("multiply", 0, 1, 4), ("meet", "x"), ("parts", 0),
     ("slab", 2, 3), ("multiply", 2, 1, 3),
     ("slab", 1, 4), ("multiply", 1, 1, 4), ("parts", 1),
     ("slab", 3, 3), ("multiply", 3, 1, 3),
@@ -25,8 +25,8 @@
     ("finish", 0), ("finish", 1), ("finish", 2), ("end",), ("finish", 3),
 )
 OTHER_PLANES = (
-    ("enter",), ("first_slab",), ("send_slab", 1), ("send_inner",), ("send_slab", 2), ("send_slab", 3),
-    ("slab", 0, 1), ("inner", 0, 1), ("slab", 1, 1), ("inner", 1, 1),
+    ("first_slab",), ("send_slab", 1), ("send_inner",), ("send_slab", 2), ("send_slab", 3),
+    ("share_inner",), ("slab", 0, 1), ("inner", 0, 1), ("slab", 1, 1), ("inner", 1, 1),
     ("slab", 2, 1), ("inner", 0, 2), ("slab", 3, 1), ("inner", 1, 2),
     ("slab", 0, 2), ("inner", 0, 3), ("slab", 1, 2), ("inner", 1, 3),
     ("inner", 0, 4), ("inner", 1, 4), ("slab", 2, 2), ("slab", 3, 2), ("wait_core",),
@@ -35,12 +35,12 @@
     ("multiply", 2, 2, 0), ("multiply", 2, 2, 1), ("multiply", 2, 2, 2),
 ) + FINISH
 FIRST_PLANE = (
-    ("enter_first",), ("first_slab",), ("send_slab", 1), ("send_slab", 2), ("send_slab", 3),
-    ("slab", 0, 1), ("meet",), ("send_inner",), ("slab", 1, 1), ("slab", 2, 1), ("slab", 3, 1),
-    ("inner", 0, 1), ("slab", 0, 2), ("inner", 1, 1), ("slab", 1, 2), ("inner", 0, 2), ("inner", 1, 2),
-    ("slab", 2, 2), ("slab", 3, 2), ("inner", 0, 3), ("slab", 0, 3), ("inner", 1, 3),
-    ("inner", 0, 4), ("slab", 1, 3), ("inner", 1, 4), ("wait_core",),
-    ("multiply", 0, 4, 0), ("multiply", 0, 4, 1), ("multiply", 0, 4, 2), ("multiply", 0, 2, 3),
+    ("first_slab",), ("send_slab", 1), ("send_slab", 2), ("send_slab", 3), ("slab", 0, 1), ("send_inner",),
+    ("share_inner",), ("slab", 1, 1), ("slab", 2, 1), ("inner", 0, 1), ("slab", 3, 1), ("inner", 1, 1),
+    ("slab", 0, 2), ("inner", 0, 2), ("slab", 1, 2), ("inner", 1, 2), ("slab", 2, 2), ("inner", 0, 3),
+    ("slab", 3, 2), ("inner", 1, 3), ("slab", 0, 3), ("inner", 0, 4), ("inner", 1, 4), ("slab", 1, 3),
+    ("wait_core",), ("multiply", 0, 4, 0), ("multiply", 0, 4, 1), ("multiply", 0, 4, 2),
+    ("multiply", 0, 2, 3),
 ) + FINISH
 
 
@@ -53,15 +53,51 @@
     z_to = [(((z + 1) % NZ) * 2 + c, y, x), (((z + NZ - 1) % NZ) * 2 + c, y, x)]
     sibling = (z * 2 + 1 - c, y, x)
     x_to = [(r, y, (x + d) % NX) for d in range(1, NX)]
+    gray = (0, 1, 3, 2)
+
+    def before(a, b, order):
+        less = [jnp.logical_and(a == i, b == k) for i in range(len(order)) for k in range(len(order))
+                if order[i] < order[k]]
+        out = less[0]
+        for term in less[1:]:
+            out = jnp.logical_or(out, term)
+        return out
+
+    z_rank = gray + tuple(range(4, NZ))
+    pairs = {
+        "core": [(sibling, c == 0)],
+        "x": [(peer, before(x, (x + d) % NX, gray)) for d, peer in enumerate(x_to, 1)],
+        "up": [(z_to[0], before(z, (z + 1) % NZ, z_rank))],
+        "down": [(z_to[1], before(z, (z + NZ - 1) % NZ, z_rank))],
+    }
+    answer = {"core": meet_sem.at[0], "x": meet_sem.at[1], "up": meet_sem.at[3], "down": meet_sem.at[2]}
+    mine = {"core": meet_sem.at[0], "x": meet_sem.at[1], "up": meet_sem.at[2], "down": meet_sem.at[3]}
+
+    def signal(sem, peer):
+        pl.semaphore_signal(sem, inc=1, device_id=peer, device_id_type=MESH)
+
     barrier = pltpu.get_barrier_semaphore()
-    for peer in y_to + [sibling] + x_to:
-        pl.semaphore_signal(barrier, inc=1, device_id=peer, device_id_type=MESH)
-    near = len(y_to) + 1 + len(x_to)
-    for step in (1, NZ - 1):
-        @pl.when(jnp.logical_and(z != 0, (z + step) % NZ != 0))
-        def _(step=step):
-            pl.semaphore_signal(
-                barrier, inc=1, device_id=(((z + step) % NZ) * 2 + c, y, x), device_id_type=MESH)
+    for peer in y_to:
+        signal(barrier, peer)
+    for kind in pairs:
+        for peer, first in pairs[kind]:
+            pl.when(first)(lambda peer=peer: signal(barrier, peer))
+
+    def count(flags):
+        return sum(jnp.where(flag, 1, 0) for flag in flags)
+
+    def enter():
+        seconds = [jnp.logical_not(first) for kind in pairs for _, first in pairs[kind]]
+        pl.semaphore_wait(barrier, len(y_to) + count(seconds))
+
+    def reply():
+        for kind in pairs:
+            for peer, first in pairs[kind]:
+                pl.when(jnp.logical_not(first))(lambda kind=kind, peer=peer: signal(answer[kind], peer))
+
+    def meet(kind):
+        firsts = count([first for _, first in pairs[kind]])
+        pl.when(firsts > 0)(lambda: pl.semaphore_wait(mine[kind], firsts))
 
     def spans(q):
         for i in range(SIDE // BW):
@@ -139,9 +175,13 @@
 
     def send_inner():
         mask_inner()
-        for p in range(PB):
-            for way in range(2):
+        for way, kind in enumerate(("up", "down")):
+            meet(kind)
+            for p in range(PB):
                 start(inner_copy(p, way, 0, 0))
+
+    def share_inner():
+        meet("core")
         for p in range(PB):
             start(core_copy(p, 0, 0, c))
 
@@ -190,32 +230,16 @@
         for copy in sends:
             copy.wait_send()
 
-    def enter_first():
+    def first_slab():
         mask_slab(0)
-        pl.semaphore_wait(barrier, near)
-        for peer in z_to:
-            pl.semaphore_signal(barrier, inc=1, device_id=peer, device_id_type=MESH)
-
-    def enter():
-        mask_slab(0)
-        pl.semaphore_wait(barrier, near + 2)
-
-        for step in (1, NZ - 1):
-            @pl.when((z + step) % NZ == 0)
-            def _(step=step):
-                pl.semaphore_signal(
-                    meet_sem, inc=1, device_id=(((z + step) % NZ) * 2 + c, y, x), device_id_type=MESH)
-
-    def meet():
-        pl.semaphore_wait(meet_sem, 2)
-
-    def first_slab():
+        enter()
         for way in range(2):
             start(slab_copy(way, 0, 0, 0))
+        reply()
 
     steps = {
-        "enter_first": enter_first, "enter": enter, "meet": meet, "first_slab": first_slab,
-        "send_slab": send_slab, "send_inner": send_inner, "slab": pass_slab, "inner": pass_inner,
+        "first_slab": first_slab, "meet": meet, "send_slab": send_slab, "send_inner": send_inner,
+        "share_inner": share_inner, "slab": pass_slab, "inner": pass_inner,
         "wait_core": wait_core, "multiply": multiply, "parts": send_parts, "finish": finish, "end": end,
     }
 
@@ -244,7 +268,7 @@
             pltpu.VMEM((NZ, SIDE, SIDE), jnp.bfloat16),
             pltpu.VMEM((NX, SIDE, 128), jnp.float32),
             pltpu.VMEM((NX - 1, SIDE, 128), jnp.float32),
-            pltpu.SemaphoreType.REGULAR,
+            pltpu.SemaphoreType.REGULAR((4,)),
             dma((Q + 1,)),
             dma((2, Q, 4)), dma((2, Q, 4)),
             dma((PB, 2, 4)), dma((PB, 2, 4)),

time: 61.8 us -> 59.9 us (0.969)
  the two profiles are of different devices: /device:TPU:64 before, /device:TPU:128 now
where the time goes in v5:
time: 59.9 us; the launch traced here: 59.8 us
  Pallas kernels  58.4 us (97%)
  local copies, waits for them, and re-layouts  1.36 us (2%)
    pallas_call x1, Pallas kernels, on_device(): pl.pallas_call(kernel, out_shape=jax.ShapeDtypeStruct((SIDE, 128), jnp.bf...  58.4 us
    unnamed x9, local copies, waits for them, and re-layouts  1.36 us

profile of v5, /device:TPU:128, one launch (start us, length us, event | category | flops | bytes accessed | tf_op | source)
XLA Modules:
  0.0 59.8 jit_solution(10925501808586930321)
XLA Ops:
  0.0 0.0 copy-start.2
  0.0 0.0 copy-start.3
  0.0 0.0 copy-start
  0.0 0.0 copy-start.1
  0.0 0.6 %copy-done.2 = s32[2]{0:T(128)S(1)} copy-done((s32[2]{0:T(128)S(1)}, s32[2]{0:T(128)}, u32[]{:S(2)}) %copy-start.2) | copy-done | bytes 32
  0.7 0.0 copy-done.3
  0.7 0.0 copy-done
  0.7 0.0 copy-done.1
  0.7 58.4 %shard_map.64 = bf16[512,128]{1,0:T(8,128)(2,1)S(1)} custom-call(bf16[512,512]{1,0:T(8,128)(2,1)} %bitcast.2, s32[2,1,2]{2,1,0:T(1,128)S(1)} %copy-done, bf16[256,512]{1,0:T(8,128)(2,1)} %bitcast.3, s32[1,1,2]{2,1,0:T(1,128)S(1)} %copy-done.1, s32[2]{0:T(128)S(1)} %copy-done.2, s32[2]{0:T(128)S(1)} %copy-done.3), custom_call_target="tpu_custom_call" | custom-call | tf_op jit(solution)/shard_map/pallas_call | solution.py:259
  59.1 0.7 %copy.8 = bf16[512,128]{1,0:T(8,128)(2,1)} copy(bf16[512,128]{1,0:T(8,128)(2,1)S(1)} %shard_map.64) | data formatting | bytes 262144
Async XLA Ops:
  0.0 0.7 %copy-start.2 = (s32[2]{0:T(128)S(1)}, s32[2]{0:T(128)}, u32[]{:S(2)}) copy-start(s32[2]{0:T(128)} %row_ids.1) | copy-start | bytes 28
  0.0 0.7 %copy-start.3 = (s32[2]{0:T(128)S(1)}, s32[2]{0:T(128)}, u32[]{:S(2)}) copy-start(s32[2]{0:T(128)} %col_ids.1) | copy-start | bytes 28
  0.0 0.7 %copy-start = (s32[2,1,2]{2,1,0:T(1,128)S(1)}, s32[2,1,2]{2,1,0:T(1,128)}, u32[]{:S(2)}) copy-start(s32[2,1,2]{2,1,0:T(1,128)} %slab_pat.1) | copy-start | bytes 52
  0.0 0.7 %copy-start.1 = (s32[1,1,2]{2,1,0:T(1,128)S(1)}, s32[1,1,2]{2,1,0:T(1,128)}, u32[]{:S(2)}) copy-start(s32[1,1,2]{2,1,0:T(1,128)} %inner_pat.1) | copy-start | bytes 28

commit v6 on v5

--- a/solution.py
+++ b/solution.py
@@ -15,33 +15,42 @@
 PB = 2
 BP = BW // PB
 
-FINISH = (
-    ("slab", 0, 4), ("multiply", 0, 1, 4), ("meet", "x"), ("parts", 0),
-    ("slab", 2, 3), ("multiply", 2, 1, 3),
-    ("slab", 1, 4), ("multiply", 1, 1, 4), ("parts", 1),
-    ("slab", 3, 3), ("multiply", 3, 1, 3),
-    ("slab", 2, 4), ("multiply", 2, 1, 4), ("parts", 2),
-    ("slab", 3, 4), ("multiply", 3, 1, 4), ("parts", 3),
-    ("finish", 0), ("finish", 1), ("finish", 2), ("end",), ("finish", 3),
+OTHER_PLANES = (
+    ("first_slab", 2), ("send_slab", 3), ("send_slab", 0), ("send_slab", 1), ("send_inner",),
+    ("share_inner",), ("slab", 2, 1), ("inner", 0, 1), ("inner", 1, 1), ("slab", 0, 1), ("slab", 3, 1),
+    ("inner", 0, 2), ("inner", 1, 2), ("slab", 2, 2), ("slab", 1, 1), ("inner", 0, 3), ("slab", 0, 2),
+    ("inner", 1, 3), ("inner", 0, 4), ("inner", 1, 4), ("slab", 2, 3), ("wait_core",), ("multiply", 0, 4, 0),
+    ("multiply", 0, 4, 1), ("multiply", 0, 1, 2), ("multiply", 2, 1, 2), ("multiply", 2, 1, 3),
+    ("slab", 1, 2), ("multiply", 1, 1, 2), ("slab", 0, 3), ("multiply", 0, 1, 3), ("slab", 3, 2),
+    ("multiply", 3, 1, 2), ("slab", 2, 4), ("multiply", 2, 1, 4), ("meet", "x"), ("parts", 2), ("slab", 1, 3),
+    ("multiply", 1, 1, 3), ("slab", 0, 4), ("multiply", 0, 1, 4), ("parts", 0), ("slab", 3, 3),
+    ("multiply", 3, 1, 3), ("slab", 1, 4), ("multiply", 1, 1, 4), ("parts", 1), ("slab", 3, 4),
+    ("multiply", 3, 1, 4), ("parts", 3), ("finish", 2), ("finish", 0), ("finish", 1), ("end",), ("finish", 3),
 )
-OTHER_PLANES = (
-    ("first_slab",), ("send_slab", 1), ("send_inner",), ("send_slab", 2), ("send_slab", 3),
-    ("share_inner",), ("slab", 0, 1), ("inner", 0, 1), ("slab", 1, 1), ("inner", 1, 1),
-    ("slab", 2, 1), ("inner", 0, 2), ("slab", 3, 1), ("inner", 1, 2),
-    ("slab", 0, 2), ("inner", 0, 3), ("slab", 1, 2), ("inner", 1, 3),
-    ("inner", 0, 4), ("inner", 1, 4), ("slab", 2, 2), ("slab", 3, 2), ("wait_core",),
-    ("multiply", 0, 2, 0), ("multiply", 0, 2, 1), ("multiply", 0, 2, 2),
-    ("slab", 0, 3), ("multiply", 0, 1, 3), ("slab", 1, 3), ("multiply", 1, 1, 3),
-    ("multiply", 2, 2, 0), ("multiply", 2, 2, 1), ("multiply", 2, 2, 2),
-) + FINISH
+NEAR_PLANES = (
+    ("first_slab", 2), ("send_slab", 3), ("send_slab", 0), ("send_slab", 1), ("send_inner",),
+    ("share_inner",), ("slab", 2, 1), ("inner", 0, 1), ("slab", 0, 1), ("slab", 3, 1), ("inner", 1, 1),
+    ("inner", 0, 2), ("slab", 2, 2), ("slab", 1, 1), ("inner", 1, 2), ("slab", 0, 2), ("inner", 0, 3),
+    ("inner", 1, 3), ("slab", 2, 3), ("inner", 0, 4), ("inner", 1, 4), ("slab", 1, 2), ("wait_core",),
+    ("multiply", 0, 4, 0), ("multiply", 0, 4, 1), ("multiply", 0, 3, 2), ("multiply", 2, 1, 3),
+    ("slab", 0, 3), ("multiply", 0, 1, 3), ("slab", 3, 2), ("multiply", 3, 1, 2), ("slab", 2, 4),
+    ("multiply", 2, 1, 4), ("meet", "x"), ("parts", 2), ("slab", 1, 3), ("multiply", 1, 1, 3), ("slab", 0, 4),
+    ("multiply", 0, 1, 4), ("parts", 0), ("slab", 3, 3), ("multiply", 3, 1, 3), ("slab", 1, 4),
+    ("multiply", 1, 1, 4), ("parts", 1), ("slab", 3, 4), ("multiply", 3, 1, 4), ("parts", 3), ("finish", 2),
+    ("finish", 0), ("finish", 1), ("end",), ("finish", 3),
+)
 FIRST_PLANE = (
-    ("first_slab",), ("send_slab", 1), ("send_slab", 2), ("send_slab", 3), ("slab", 0, 1), ("send_inner",),
-    ("share_inner",), ("slab", 1, 1), ("slab", 2, 1), ("inner", 0, 1), ("slab", 3, 1), ("inner", 1, 1),
-    ("slab", 0, 2), ("inner", 0, 2), ("slab", 1, 2), ("inner", 1, 2), ("slab", 2, 2), ("inner", 0, 3),
-    ("slab", 3, 2), ("inner", 1, 3), ("slab", 0, 3), ("inner", 0, 4), ("inner", 1, 4), ("slab", 1, 3),
-    ("wait_core",), ("multiply", 0, 4, 0), ("multiply", 0, 4, 1), ("multiply", 0, 4, 2),
-    ("multiply", 0, 2, 3),
-) + FINISH
+    ("first_slab", 2), ("send_slab", 3), ("send_slab", 0), ("send_slab", 1), ("send_inner",),
+    ("share_inner",), ("slab", 2, 1), ("slab", 0, 1), ("slab", 3, 1), ("inner", 0, 1), ("inner", 1, 1),
+    ("slab", 2, 2), ("slab", 1, 1), ("inner", 0, 2), ("slab", 0, 2), ("inner", 1, 2), ("inner", 0, 3),
+    ("slab", 2, 3), ("inner", 1, 3), ("slab", 1, 2), ("inner", 0, 4), ("inner", 1, 4), ("slab", 0, 3),
+    ("slab", 3, 2), ("wait_core",), ("multiply", 0, 4, 0), ("multiply", 0, 4, 1), ("multiply", 0, 4, 2),
+    ("multiply", 0, 1, 3), ("multiply", 2, 1, 3), ("slab", 2, 4), ("multiply", 2, 1, 4), ("meet", "x"),
+    ("parts", 2), ("slab", 1, 3), ("multiply", 1, 1, 3), ("slab", 0, 4), ("multiply", 0, 1, 4), ("parts", 0),
+    ("slab", 3, 3), ("multiply", 3, 1, 3), ("slab", 1, 4), ("multiply", 1, 1, 4), ("parts", 1),
+    ("slab", 3, 4), ("multiply", 3, 1, 4), ("parts", 3), ("finish", 2), ("finish", 0), ("finish", 1),
+    ("end",), ("finish", 3),
+)
 
 
 def kernel(slab, slab_pat, inner, inner_pat, row_ids, col_ids, out,
@@ -230,11 +239,11 @@
         for copy in sends:
             copy.wait_send()
 
-    def first_slab():
-        mask_slab(0)
+    def first_slab(q):
+        mask_slab(q)
         enter()
         for way in range(2):
-            start(slab_copy(way, 0, 0, 0))
+            start(slab_copy(way, q, 0, 0))
         reply()
 
     steps = {
@@ -249,7 +258,8 @@
             steps[name](*args)
 
     pl.when(z == 0)(lambda: run(FIRST_PLANE))
-    pl.when(z != 0)(lambda: run(OTHER_PLANES))
+    pl.when(jnp.logical_and(z > 0, z <= 2))(lambda: run(NEAR_PLANES))
+    pl.when(z > 2)(lambda: run(OTHER_PLANES))
 
 
 def on_device(slab_panel, slab_pattern, inner_panel, inner_pattern, slab_rows, column_ids):

time: 59.9 us -> 57.9 us (0.967)
  the two profiles are of different devices: /device:TPU:128 before, /device:TPU:1 now
where the time goes in v6:
time: 57.9 us; the launch traced here: 57.4 us
  Pallas kernels  56.1 us (97%)
  local copies, waits for them, and re-layouts  1.36 us (2%)
    pallas_call x1, Pallas kernels, on_device(): pl.pallas_call(kernel, out_shape=jax.ShapeDtypeStruct((SIDE, 128), jnp.bf...  56.1 us
    unnamed x9, local copies, waits for them, and re-layouts  1.36 us

profile of v6, /device:TPU:1, one launch (start us, length us, event | category | flops | bytes accessed | tf_op | source)
XLA Modules:
  0.0 57.4 jit_solution(8897809677196458482)
XLA Ops:
  0.0 0.0 copy-start.2
  0.0 0.0 copy-start.3
  0.0 0.0 copy-start
  0.0 0.0 copy-start.1
  0.0 0.6 %copy-done.2 = s32[2]{0:T(128)S(1)} copy-done((s32[2]{0:T(128)S(1)}, s32[2]{0:T(128)}, u32[]{:S(2)}) %copy-start.2) | copy-done | bytes 32
  0.7 0.0 copy-done.3
  0.7 0.0 copy-done
  0.7 0.0 copy-done.1
  0.7 56.1 %shard_map.64 = bf16[512,128]{1,0:T(8,128)(2,1)S(1)} custom-call(bf16[512,512]{1,0:T(8,128)(2,1)} %bitcast.2, s32[2,1,2]{2,1,0:T(1,128)S(1)} %copy-done, bf16[256,512]{1,0:T(8,128)(2,1)} %bitcast.3, s32[1,1,2]{2,1,0:T(1,128)S(1)} %copy-done.1, s32[2]{0:T(128)S(1)} %copy-done.2, s32[2]{0:T(128)S(1)} %copy-done.3), custom_call_target="tpu_custom_call" | custom-call | tf_op jit(solution)/shard_map/pallas_call | solution.py:269
  56.8 0.7 %copy.8 = bf16[512,128]{1,0:T(8,128)(2,1)} copy(bf16[512,128]{1,0:T(8,128)(2,1)S(1)} %shard_map.64) | data formatting | bytes 262144
Async XLA Ops:
  0.0 0.7 %copy-start.2 = (s32[2]{0:T(128)S(1)}, s32[2]{0:T(128)}, u32[]{:S(2)}) copy-start(s32[2]{0:T(128)} %row_ids.1) | copy-start | bytes 28
  0.0 0.7 %copy-start.3 = (s32[2]{0:T(128)S(1)}, s32[2]{0:T(128)}, u32[]{:S(2)}) copy-start(s32[2]{0:T(128)} %col_ids.1) | copy-start | bytes 28
  0.0 0.7 %copy-start = (s32[2,1,2]{2,1,0:T(1,128)S(1)}, s32[2,1,2]{2,1,0:T(1,128)}, u32[]{:S(2)}) copy-start(s32[2,1,2]{2,1,0:T(1,128)} %slab_pat.1) | copy-start | bytes 52
  0.0 0.7 %copy-start.1 = (s32[1,1,2]{2,1,0:T(1,128)S(1)}, s32[1,1,2]{2,1,0:T(1,128)}, u32[]{:S(2)}) copy-start(s32[1,1,2]{2,1,0:T(1,128)} %inner_pat.1) | copy-start | bytes 28

commit v7 on v6

--- a/solution.py
+++ b/solution.py
@@ -15,41 +15,44 @@
 PB = 2
 BP = BW // PB
 
+FIRST_SLAB, SEND_SLAB, SEND_INNER, SHARE_INNER, SLAB, INNER, \
+    WAIT_CORE, MULTIPLY, MEET, PARTS, FINISH, END = range(12)
+CORE, X, UP, DOWN = range(4)
 OTHER_PLANES = (
-    ("first_slab", 2), ("send_slab", 3), ("send_slab", 0), ("send_slab", 1), ("send_inner",),
-    ("share_inner",), ("slab", 2, 1), ("inner", 0, 1), ("inner", 1, 1), ("slab", 0, 1), ("slab", 3, 1),
-    ("inner", 0, 2), ("inner", 1, 2), ("slab", 2, 2), ("slab", 1, 1), ("inner", 0, 3), ("slab", 0, 2),
-    ("inner", 1, 3), ("inner", 0, 4), ("inner", 1, 4), ("slab", 2, 3), ("wait_core",), ("multiply", 0, 4, 0),
-    ("multiply", 0, 4, 1), ("multiply", 0, 1, 2), ("multiply", 2, 1, 2), ("multiply", 2, 1, 3),
-    ("slab", 1, 2), ("multiply", 1, 1, 2), ("slab", 0, 3), ("multiply", 0, 1, 3), ("slab", 3, 2),
-    ("multiply", 3, 1, 2), ("slab", 2, 4), ("multiply", 2, 1, 4), ("meet", "x"), ("parts", 2), ("slab", 1, 3),
-    ("multiply", 1, 1, 3), ("slab", 0, 4), ("multiply", 0, 1, 4), ("parts", 0), ("slab", 3, 3),
-    ("multiply", 3, 1, 3), ("slab", 1, 4), ("multiply", 1, 1, 4), ("parts", 1), ("slab", 3, 4),
-    ("multiply", 3, 1, 4), ("parts", 3), ("finish", 2), ("finish", 0), ("finish", 1), ("end",), ("finish", 3),
+    (FIRST_SLAB, 2), (SEND_SLAB, 3), (SEND_SLAB, 0), (SEND_SLAB, 1), (SEND_INNER,),
+    (SHARE_INNER,), (SLAB, 2, 1), (INNER, 0, 1), (INNER, 1, 1), (SLAB, 0, 1), (SLAB, 3, 1),
+    (INNER, 0, 2), (INNER, 1, 2), (SLAB, 2, 2), (SLAB, 1, 1), (INNER, 0, 3), (SLAB, 0, 2),
+    (INNER, 1, 3), (INNER, 0, 4), (INNER, 1, 4), (SLAB, 2, 3), (WAIT_CORE,), (MULTIPLY, 0, 4, 0),
+    (MULTIPLY, 0, 4, 1), (MULTIPLY, 0, 1, 2), (MULTIPLY, 2, 1, 2), (MULTIPLY, 2, 1, 3),
+    (SLAB, 1, 2), (MULTIPLY, 1, 1, 2), (SLAB, 0, 3), (MULTIPLY, 0, 1, 3), (SLAB, 3, 2),
+    (MULTIPLY, 3, 1, 2), (SLAB, 2, 4), (MULTIPLY, 2, 1, 4), (MEET, X), (PARTS, 2), (SLAB, 1, 3),
+    (MULTIPLY, 1, 1, 3), (SLAB, 0, 4), (MULTIPLY, 0, 1, 4), (PARTS, 0), (SLAB, 3, 3),
+    (MULTIPLY, 3, 1, 3), (SLAB, 1, 4), (MULTIPLY, 1, 1, 4), (PARTS, 1), (SLAB, 3, 4),
+    (MULTIPLY, 3, 1, 4), (PARTS, 3), (FINISH, 2), (FINISH, 0), (FINISH, 1), (END,), (FINISH, 3),
 )
 NEAR_PLANES = (
-    ("first_slab", 2), ("send_slab", 3), ("send_slab", 0), ("send_slab", 1), ("send_inner",),
-    ("share_inner",), ("slab", 2, 1), ("inner", 0, 1), ("slab", 0, 1), ("slab", 3, 1), ("inner", 1, 1),
-    ("inner", 0, 2), ("slab", 2, 2), ("slab", 1, 1), ("inner", 1, 2), ("slab", 0, 2), ("inner", 0, 3),
-    ("inner", 1, 3), ("slab", 2, 3), ("inner", 0, 4), ("inner", 1, 4), ("slab", 1, 2), ("wait_core",),
-    ("multiply", 0, 4, 0), ("multiply", 0, 4, 1), ("multiply", 0, 3, 2), ("multiply", 2, 1, 3),
-    ("slab", 0, 3), ("multiply", 0, 1, 3), ("slab", 3, 2), ("multiply", 3, 1, 2), ("slab", 2, 4),
-    ("multiply", 2, 1, 4), ("meet", "x"), ("parts", 2), ("slab", 1, 3), ("multiply", 1, 1, 3), ("slab", 0, 4),
-    ("multiply", 0, 1, 4), ("parts", 0), ("slab", 3, 3), ("multiply", 3, 1, 3), ("slab", 1, 4),
-    ("multiply", 1, 1, 4), ("parts", 1), ("slab", 3, 4), ("multiply", 3, 1, 4), ("parts", 3), ("finish", 2),
-    ("finish", 0), ("finish", 1), ("end",), ("finish", 3),
+    (FIRST_SLAB, 2), (SEND_SLAB, 3), (SEND_SLAB, 0), (SEND_SLAB, 1), (SEND_INNER,),
+    (SHARE_INNER,), (SLAB, 2, 1), (INNER, 0, 1), (SLAB, 0, 1), (SLAB, 3, 1), (INNER, 1, 1),
+    (INNER, 0, 2), (SLAB, 2, 2), (SLAB, 1, 1), (INNER, 1, 2), (SLAB, 0, 2), (INNER, 0, 3),
+    (INNER, 1, 3), (SLAB, 2, 3), (INNER, 0, 4), (INNER, 1, 4), (SLAB, 1, 2), (WAIT_CORE,),
+    (MULTIPLY, 0, 4, 0), (MULTIPLY, 0, 4, 1), (MULTIPLY, 0, 3, 2), (MULTIPLY, 2, 1, 3),
+    (SLAB, 0, 3), (MULTIPLY, 0, 1, 3), (SLAB, 3, 2), (MULTIPLY, 3, 1, 2), (SLAB, 2, 4),
+    (MULTIPLY, 2, 1, 4), (MEET, X), (PARTS, 2), (SLAB, 1, 3), (MULTIPLY, 1, 1, 3), (SLAB, 0, 4),
+    (MULTIPLY, 0, 1, 4), (PARTS, 0), (SLAB, 3, 3), (MULTIPLY, 3, 1, 3), (SLAB, 1, 4),
+    (MULTIPLY, 1, 1, 4), (PARTS, 1), (SLAB, 3, 4), (MULTIPLY, 3, 1, 4), (PARTS, 3), (FINISH, 2),
+    (FINISH, 0), (FINISH, 1), (END,), (FINISH, 3),
 )
 FIRST_PLANE = (
-    ("first_slab", 2), ("send_slab", 3), ("send_slab", 0), ("send_slab", 1), ("send_inner",),
-    ("share_inner",), ("slab", 2, 1), ("slab", 0, 1), ("slab", 3, 1), ("inner", 0, 1), ("inner", 1, 1),
-    ("slab", 2, 2), ("slab", 1, 1), ("inner", 0, 2), ("slab", 0, 2), ("inner", 1, 2), ("inner", 0, 3),
-    ("slab", 2, 3), ("inner", 1, 3), ("slab", 1, 2), ("inner", 0, 4), ("inner", 1, 4), ("slab", 0, 3),
-    ("slab", 3, 2), ("wait_core",), ("multiply", 0, 4, 0), ("multiply", 0, 4, 1), ("multiply", 0, 4, 2),
-    ("multiply", 0, 1, 3), ("multiply", 2, 1, 3), ("slab", 2, 4), ("multiply", 2, 1, 4), ("meet", "x"),
-    ("parts", 2), ("slab", 1, 3), ("multiply", 1, 1, 3), ("slab", 0, 4), ("multiply", 0, 1, 4), ("parts", 0),
-    ("slab", 3, 3), ("multiply", 3, 1, 3), ("slab", 1, 4), ("multiply", 1, 1, 4), ("parts", 1),
-    ("slab", 3, 4), ("multiply", 3, 1, 4), ("parts", 3), ("finish", 2), ("finish", 0), ("finish", 1),
-    ("end",), ("finish", 3),
+    (FIRST_SLAB, 2), (SEND_SLAB, 3), (SEND_SLAB, 0), (SEND_SLAB, 1), (SEND_INNER,),
+    (SHARE_INNER,), (SLAB, 2, 1), (SLAB, 0, 1), (SLAB, 3, 1), (INNER, 0, 1), (INNER, 1, 1),
+    (SLAB, 2, 2), (SLAB, 1, 1), (INNER, 0, 2), (SLAB, 0, 2), (INNER, 1, 2), (INNER, 0, 3),
+    (SLAB, 2, 3), (INNER, 1, 3), (SLAB, 1, 2), (INNER, 0, 4), (INNER, 1, 4), (SLAB, 0, 3),
+    (SLAB, 3, 2), (WAIT_CORE,), (MULTIPLY, 0, 4, 0), (MULTIPLY, 0, 4, 1), (MULTIPLY, 0, 4, 2),
+    (MULTIPLY, 0, 1, 3), (MULTIPLY, 2, 1, 3), (SLAB, 2, 4), (MULTIPLY, 2, 1, 4), (MEET, X),
+    (PARTS, 2), (SLAB, 1, 3), (MULTIPLY, 1, 1, 3), (SLAB, 0, 4), (MULTIPLY, 0, 1, 4), (PARTS, 0),
+    (SLAB, 3, 3), (MULTIPLY, 3, 1, 3), (SLAB, 1, 4), (MULTIPLY, 1, 1, 4), (PARTS, 1),
+    (SLAB, 3, 4), (MULTIPLY, 3, 1, 4), (PARTS, 3), (FINISH, 2), (FINISH, 0), (FINISH, 1),
+    (END,), (FINISH, 3),
 )
 
 
@@ -74,13 +77,13 @@
 
     z_rank = gray + tuple(range(4, NZ))
     pairs = {
-        "core": [(sibling, c == 0)],
-        "x": [(peer, before(x, (x + d) % NX, gray)) for d, peer in enumerate(x_to, 1)],
-        "up": [(z_to[0], before(z, (z + 1) % NZ, z_rank))],
-        "down": [(z_to[1], before(z, (z + NZ - 1) % NZ, z_rank))],
+        CORE: [(sibling, c == 0)],
+        X: [(peer, before(x, (x + d) % NX, gray)) for d, peer in enumerate(x_to, 1)],
+        UP: [(z_to[0], before(z, (z + 1) % NZ, z_rank))],
+        DOWN: [(z_to[1], before(z, (z + NZ - 1) % NZ, z_rank))],
     }
-    answer = {"core": meet_sem.at[0], "x": meet_sem.at[1], "up": meet_sem.at[3], "down": meet_sem.at[2]}
-    mine = {"core": meet_sem.at[0], "x": meet_sem.at[1], "up": meet_sem.at[2], "down": meet_sem.at[3]}
+    answer = {CORE: meet_sem.at[0], X: meet_sem.at[1], UP: meet_sem.at[3], DOWN: meet_sem.at[2]}
+    mine = {CORE: meet_sem.at[0], X: meet_sem.at[1], UP: meet_sem.at[2], DOWN: meet_sem.at[3]}
 
     def signal(sem, peer):
         pl.semaphore_signal(sem, inc=1, device_id=peer, device_id_type=MESH)
@@ -184,13 +187,13 @@
 
     def send_inner():
         mask_inner()
-        for way, kind in enumerate(("up", "down")):
+        for way, kind in enumerate((UP, DOWN)):
             meet(kind)
             for p in range(PB):
                 start(inner_copy(p, way, 0, 0))
 
     def share_inner():
-        meet("core")
+        meet(CORE)
         for p in range(PB):
             start(core_copy(p, 0, 0, c))
 
@@ -247,9 +250,9 @@
         reply()
 
     steps = {
-        "first_slab": first_slab, "meet": meet, "send_slab": send_slab, "send_inner": send_inner,
-        "share_inner": share_inner, "slab": pass_slab, "inner": pass_inner,
-        "wait_core": wait_core, "multiply": multiply, "parts": send_parts, "finish": finish, "end": end,
+        FIRST_SLAB: first_slab, SEND_SLAB: send_slab, SEND_INNER: send_inner, SHARE_INNER: share_inner,
+        SLAB: pass_slab, INNER: pass_inner, WAIT_CORE: wait_core, MULTIPLY: multiply, MEET: meet,
+        PARTS: send_parts, FINISH: finish, END: end,
     }
 
     def run(schedule):

time: 57.9 us -> 57.9 us (level)
  no operation moved by 1% of the time
where the time goes in v7:
time: 57.9 us; the launch traced here: 57.4 us
  Pallas kernels  56.1 us (97%)
  local copies, waits for them, and re-layouts  1.36 us (2%)
    pallas_call x1, Pallas kernels, on_device(): pl.pallas_call(kernel, out_shape=jax.ShapeDtypeStruct((SIDE, 128), jnp.bf...  56.1 us
    unnamed x9, local copies, waits for them, and re-layouts  1.36 us

profile of v7, /device:TPU:1, one launch (start us, length us, event | category | flops | bytes accessed | tf_op | source)
XLA Modules:
  0.0 57.4 jit_solution(8897809677196458482)
XLA Ops:
  0.0 0.0 copy-start.2
  0.0 0.0 copy-start.3
  0.0 0.0 copy-start
  0.0 0.0 copy-start.1
  0.0 0.6 %copy-done.2 = s32[2]{0:T(128)S(1)} copy-done((s32[2]{0:T(128)S(1)}, s32[2]{0:T(128)}, u32[]{:S(2)}) %copy-start.2) | copy-done | bytes 32
  0.7 0.0 copy-done.3
  0.7 0.0 copy-done
  0.7 0.0 copy-done.1
  0.7 56.1 %shard_map.64 = bf16[512,128]{1,0:T(8,128)(2,1)S(1)} custom-call(bf16[512,512]{1,0:T(8,128)(2,1)} %bitcast.2, s32[2,1,2]{2,1,0:T(1,128)S(1)} %copy-done, bf16[256,512]{1,0:T(8,128)(2,1)} %bitcast.3, s32[1,1,2]{2,1,0:T(1,128)S(1)} %copy-done.1, s32[2]{0:T(128)S(1)} %copy-done.2, s32[2]{0:T(128)S(1)} %copy-done.3), custom_call_target="tpu_custom_call" | custom-call | tf_op jit(solution)/shard_map/pallas_call | solution.py:272
  56.8 0.7 %copy.8 = bf16[512,128]{1,0:T(8,128)(2,1)} copy(bf16[512,128]{1,0:T(8,128)(2,1)S(1)} %shard_map.64) | data formatting | bytes 262144
Async XLA Ops:
  0.0 0.7 %copy-start.2 = (s32[2]{0:T(128)S(1)}, s32[2]{0:T(128)}, u32[]{:S(2)}) copy-start(s32[2]{0:T(128)} %row_ids.1) | copy-start | bytes 28
  0.0 0.7 %copy-start.3 = (s32[2]{0:T(128)S(1)}, s32[2]{0:T(128)}, u32[]{:S(2)}) copy-start(s32[2]{0:T(128)} %col_ids.1) | copy-start | bytes 28
  0.0 0.7 %copy-start = (s32[2,1,2]{2,1,0:T(1,128)S(1)}, s32[2,1,2]{2,1,0:T(1,128)}, u32[]{:S(2)}) copy-start(s32[2,1,2]{2,1,0:T(1,128)} %slab_pat.1) | copy-start | bytes 52
  0.0 0.7 %copy-start.1 = (s32[1,1,2]{2,1,0:T(1,128)S(1)}, s32[1,1,2]{2,1,0:T(1,128)}, u32[]{:S(2)}) copy-start(s32[1,1,2]{2,1,0:T(1,128)} %inner_pat.1) | copy-start | bytes 28

commit v8 on v7

--- a/solution.py
+++ b/solution.py
@@ -27,8 +27,8 @@
     (SLAB, 1, 2), (MULTIPLY, 1, 1, 2), (SLAB, 0, 3), (MULTIPLY, 0, 1, 3), (SLAB, 3, 2),
     (MULTIPLY, 3, 1, 2), (SLAB, 2, 4), (MULTIPLY, 2, 1, 4), (MEET, X), (PARTS, 2), (SLAB, 1, 3),
     (MULTIPLY, 1, 1, 3), (SLAB, 0, 4), (MULTIPLY, 0, 1, 4), (PARTS, 0), (SLAB, 3, 3),
-    (MULTIPLY, 3, 1, 3), (SLAB, 1, 4), (MULTIPLY, 1, 1, 4), (PARTS, 1), (SLAB, 3, 4),
-    (MULTIPLY, 3, 1, 4), (PARTS, 3), (FINISH, 2), (FINISH, 0), (FINISH, 1), (END,), (FINISH, 3),
+    (MULTIPLY, 3, 1, 3), (SLAB, 1, 4), (MULTIPLY, 1, 1, 4), (PARTS, 1), (FINISH, 2), (SLAB, 3, 4),
+    (MULTIPLY, 3, 1, 4), (PARTS, 3),  (FINISH, 0), (FINISH, 1), (END,), (FINISH, 3),
 )
 NEAR_PLANES = (
     (FIRST_SLAB, 2), (SEND_SLAB, 3), (SEND_SLAB, 0), (SEND_SLAB, 1), (SEND_INNER,),
@@ -39,7 +39,7 @@
     (SLAB, 0, 3), (MULTIPLY, 0, 1, 3), (SLAB, 3, 2), (MULTIPLY, 3, 1, 2), (SLAB, 2, 4),
     (MULTIPLY, 2, 1, 4), (MEET, X), (PARTS, 2), (SLAB, 1, 3), (MULTIPLY, 1, 1, 3), (SLAB, 0, 4),
     (MULTIPLY, 0, 1, 4), (PARTS, 0), (SLAB, 3, 3), (MULTIPLY, 3, 1, 3), (SLAB, 1, 4),
-    (MULTIPLY, 1, 1, 4), (PARTS, 1), (SLAB, 3, 4), (MULTIPLY, 3, 1, 4), (PARTS, 3), (FINISH, 2),
+    (MULTIPLY, 1, 1, 4), (PARTS, 1), (FINISH, 2), (SLAB, 3, 4), (MULTIPLY, 3, 1, 4), (PARTS, 3),
     (FINISH, 0), (FINISH, 1), (END,), (FINISH, 3),
 )
 FIRST_PLANE = (
@@ -50,8 +50,8 @@
     (SLAB, 3, 2), (WAIT_CORE,), (MULTIPLY, 0, 4, 0), (MULTIPLY, 0, 4, 1), (MULTIPLY, 0, 4, 2),
     (MULTIPLY, 0, 1, 3), (MULTIPLY, 2, 1, 3), (SLAB, 2, 4), (MULTIPLY, 2, 1, 4), (MEET, X),
     (PARTS, 2), (SLAB, 1, 3), (MULTIPLY, 1, 1, 3), (SLAB, 0, 4), (MULTIPLY, 0, 1, 4), (PARTS, 0),
-    (SLAB, 3, 3), (MULTIPLY, 3, 1, 3), (SLAB, 1, 4), (MULTIPLY, 1, 1, 4), (PARTS, 1),
-    (SLAB, 3, 4), (MULTIPLY, 3, 1, 4), (PARTS, 3), (FINISH, 2), (FINISH, 0), (FINISH, 1),
+    (SLAB, 3, 3), (MULTIPLY, 3, 1, 3), (SLAB, 1, 4), (MULTIPLY, 1, 1, 4), (PARTS, 1), (FINISH, 2),
+    (SLAB, 3, 4), (MULTIPLY, 3, 1, 4), (PARTS, 3),  (FINISH, 0), (FINISH, 1),
     (END,), (FINISH, 3),
 )
 

time: 57.9 us -> 57.9 us (level)
  no operation moved by 1% of the time
where the time goes in v8:
time: 57.9 us; the launch traced here: 57.4 us
  Pallas kernels  56.1 us (97%)
  local copies, waits for them, and re-layouts  1.36 us (2%)
    pallas_call x1, Pallas kernels, on_device(): pl.pallas_call(kernel, out_shape=jax.ShapeDtypeStruct((SIDE, 128), jnp.bf...  56.1 us
    unnamed x9, local copies, waits for them, and re-layouts  1.36 us

profile of v8, /device:TPU:1, one launch (start us, length us, event | category | flops | bytes accessed | tf_op | source)
XLA Modules:
  0.0 57.4 jit_solution(6463084902165671578)
XLA Ops:
  0.0 0.0 copy-start.2
  0.0 0.0 copy-start.3
  0.0 0.0 copy-start
  0.0 0.0 copy-start.1
  0.0 0.6 %copy-done.2 = s32[2]{0:T(128)S(1)} copy-done((s32[2]{0:T(128)S(1)}, s32[2]{0:T(128)}, u32[]{:S(2)}) %copy-start.2) | copy-done | bytes 32
  0.7 0.0 copy-done.3
  0.7 0.0 copy-done
  0.7 0.0 copy-done.1
  0.7 56.1 %shard_map.64 = bf16[512,128]{1,0:T(8,128)(2,1)S(1)} custom-call(bf16[512,512]{1,0:T(8,128)(2,1)} %bitcast.2, s32[2,1,2]{2,1,0:T(1,128)S(1)} %copy-done, bf16[256,512]{1,0:T(8,128)(2,1)} %bitcast.3, s32[1,1,2]{2,1,0:T(1,128)S(1)} %copy-done.1, s32[2]{0:T(128)S(1)} %copy-done.2, s32[2]{0:T(128)S(1)} %copy-done.3), custom_call_target="tpu_custom_call" | custom-call | tf_op jit(solution)/shard_map/pallas_call | solution.py:272
  56.8 0.7 %copy.8 = bf16[512,128]{1,0:T(8,128)(2,1)} copy(bf16[512,128]{1,0:T(8,128)(2,1)S(1)} %shard_map.64) | data formatting | bytes 262144
Async XLA Ops:
  0.0 0.7 %copy-start.2 = (s32[2]{0:T(128)S(1)}, s32[2]{0:T(128)}, u32[]{:S(2)}) copy-start(s32[2]{0:T(128)} %row_ids.1) | copy-start | bytes 28
  0.0 0.7 %copy-start.3 = (s32[2]{0:T(128)S(1)}, s32[2]{0:T(128)}, u32[]{:S(2)}) copy-start(s32[2]{0:T(128)} %col_ids.1) | copy-start | bytes 28
  0.0 0.7 %copy-start = (s32[2,1,2]{2,1,0:T(1,128)S(1)}, s32[2,1,2]{2,1,0:T(1,128)}, u32[]{:S(2)}) copy-start(s32[2,1,2]{2,1,0:T(1,128)} %slab_pat.1) | copy-start | bytes 52
  0.0 0.7 %copy-start.1 = (s32[1,1,2]{2,1,0:T(1,128)S(1)}, s32[1,1,2]{2,1,0:T(1,128)}, u32[]{:S(2)}) copy-start(s32[1,1,2]{2,1,0:T(1,128)} %inner_pat.1) | copy-start | bytes 28
